TPU v7x, 512 devices: a whole 4x4x16 slice. The times are simulated.
512 devices in a mesh: dp: 32 (over y, z_hi, core), shard: 16 (over x, z_lo).
Axes of the slice: x: 4, y: 4, z: 16 (z_hi: 4, z_lo: 4; z = z_hi * 4 + z_lo), core: 2. Of those that a mesh axis runs over, the one named last changes fastest.
Arguments:
- ffn_input: bfloat16 [16384, 8192], P('dp', 'shard'), may hold values from -6 to 6
- up_cotangent: bfloat16 [16384, 28672], P('dp', 'shard'), may hold values from -0.059814453 to 0.059814453
- projector: bfloat16 [8192, 512], P('shard'), may hold values from -0.0625 to 0.0625
- first_moment: float32 [512, 28672], P('dp', 'shard'), may hold values from -0.6 to 0.6
- second_moment: float32 [512, 28672], P('dp', 'shard'), may hold values from 0.0001 to 0.01
Outputs:
- expanded_step: bfloat16 [8192, 28672], P('dp', 'shard')
- first_next: float32 [512, 28672], P('dp', 'shard')
- second_next: float32 [512, 28672], P('dp', 'shard')
All inputs are finite; a program needn't handle non-finite values.
Results may differ from a plain program's by a relative error of at most 0.0061.
Values may be sent and summed in bfloat16 or wider, within the bound.
No kernel may reach another device: no remote copies, remote signals or barrier semaphores. Data moves between devices by JAX's collectives and lax.ppermute only.
A program may use at most 64 MiB of HBM per device.

v0:
```python
import jax
import jax.numpy as jnp
from jax import lax
from jax.sharding import PartitionSpec as P

D = 8192
STEP = 10


beta_first = 0.9
beta_second = 0.999
epsilon = 1e-08


def fetch_rows(projector):
    rows_dp = D // lax.axis_size("dp")
    whole_basis = lax.all_gather(projector, "shard", axis=0, tiled=True)
    return lax.dynamic_slice_in_dim(whole_basis, lax.axis_index("dp") * rows_dp, rows_dp, 0)


def adam_update(low_grad, first_moment, second_moment):
    first_next = beta_first * first_moment + (1.0 - beta_first) * low_grad
    second_next = beta_second * second_moment + (1.0 - beta_second) * low_grad * low_grad
    first_hat = first_next / (1.0 - beta_first**STEP)
    second_hat = second_next / (1.0 - beta_second**STEP)
    normalized = (first_hat / (jnp.sqrt(second_hat) + epsilon)).astype(jnp.bfloat16)
    return (first_next, second_next, normalized)


def on_device(ffn_input, up_cotangent, projector, first_moment, second_moment):
    local_proj = jnp.dot(ffn_input, projector, preferred_element_type=jnp.float32)
    projected = lax.psum(local_proj, "shard").astype(jnp.bfloat16)
    low_grad = lax.psum_scatter(
        lax.dot_general(
            projected, up_cotangent, (((0,), (0,)), ((), ())), preferred_element_type=jnp.float32
        ),
        "dp",
        scatter_dimension=0,
        tiled=True,
    )
    first_next, second_next, normalized = adam_update(low_grad, first_moment, second_moment)
    full_step = lax.all_gather(normalized, "dp", axis=0, tiled=True)
    basis_rows = fetch_rows(projector)
    expanded_step = jnp.dot(basis_rows, full_step, preferred_element_type=jnp.float32).astype(
        jnp.bfloat16
    )
    return (expanded_step, first_next, second_next)


def solution(mesh):
    in_specs = (
        P("dp", "shard"),
        P("dp", "shard"),
        P("shard", None),
        P("dp", "shard"),
        P("dp", "shard"),
    )
    out_specs = (P("dp", "shard"), P("dp", "shard"), P("dp", "shard"))
    return jax.shard_map(
        on_device, mesh=mesh, in_specs=in_specs, out_specs=out_specs, check_vma=False
    )
```

profile of v0, /device:TPU:1, one launch (start us, length us, event | category | flops | bytes accessed | tf_op | source)
XLA Modules:
  0.0 521.9 jit_solution(8071187930282746703)
XLA Ops:
  7.2 0.0 copy-start
  7.2 0.0 reduce-scatter.2.cloned.1.call-start
  7.2 1.8 fusion.6
  9.0 89.5 %all-reduce.1 = bf16[512,512]{1,0:T(8,128)(2,1)S(1)} all-reduce(f32[512,512]{1,0:T(8,128)S(1)} %fusion.6), channel_id=1, replica_groups=mesh['dp'=32,'shard'=16] {'shard'}, use_global_device_ids=true, to_apply=%region_0.0 | all-reduce | flops 262144 | bytes 1572864 | tf_op jit(solution)/shard_map/psum | solution.py:32
  98.5 0.0 copy-done
  98.5 2.9 fusion.7
  101.4 0.0 copy-start.1
  101.4 0.0 copy-start.2
  101.4 0.0 reduce-scatter.2.cloned.1.call-update
  101.4 0.0 all-gather.5.cloned.1.call-start
  101.5 145.6 %reduce-scatter.2.cloned.1.call-done = f32[16,1792]{1,0:T(8,128)} async-done(((f32[512,1792]{1,0:T(8,128)}), f32[16,1792]{1,0:T(8,128)}) %reduce-scatter.2.cloned.1.call-update) | async-done | bytes 114704 | tf_op jit(solution)/shard_map/reduce_scatter | solution.py:33
  247.1 0.0 copy-done.1
  247.1 0.0 copy-done.2
  247.1 1.6 divide_convert_fusion
  248.7 0.0 all-gather.5.cloned.1.call-update
  248.8 0.0 all-gather.3.cloned.1.call-start
  248.8 0.7 all-gather.3.cloned.1.call-update
  249.5 74.2 %all-gather.5.cloned.1.call-done = bf16[512,1792]{1,0:T(8,128)(2,1)} async-done(((bf16[16,1792]{1,0:T(8,128)(2,1)}), bf16[512,1792]{1,0:T(8,128)(2,1)}) %all-gather.5.cloned.1.call-update) | async-done | bytes 1835024 | tf_op jit(solution)/shard_map/all_gather | solution.py:42
  323.7 188.5 %all-gather.3.cloned.1.call-done = bf16[8192,512]{1,0:T(8,128)(2,1)} async-done(((bf16[512,512]{1,0:T(8,128)(2,1)}), bf16[8192,512]{1,0:T(8,128)(2,1)}) %all-gather.3.cloned.1.call-update) | async-done | bytes 8388624 | tf_op jit(solution)/shard_map/all_gather | solution.py:17
  512.2 3.2 convolution_convert_fusion
Async XLA Ops:
  7.2 91.3 %copy-start = (bf16[512,1792]{1,0:T(8,128)(2,1)S(1)}, bf16[512,1792]{1,0:T(8,128)(2,1)}, u32[]{:S(2)}) copy-start(bf16[512,1792]{1,0:T(8,128)(2,1)} %param.6) | copy-start | bytes 5505028
  7.2 239.9 %reduce-scatter.2.cloned.1.call-start = ((), (), s32[]{:S(2)}) async-start(), calls=%async_computation.2 | async-start | bytes 3784704 | tf_op jit(solution)/shard_map/reduce_scatter | solution.py:33
  101.4 145.7 %copy-start.1 = (f32[16,1792]{1,0:T(8,128)S(1)}, f32[16,1792]{1,0:T(8,128)}, u32[]{:S(2)}) copy-start(f32[16,1792]{1,0:T(8,128)} %param.8) | copy-start | bytes 344068
  101.4 145.7 %copy-start.2 = (f32[16,1792]{1,0:T(8,128)S(1)}, f32[16,1792]{1,0:T(8,128)}, u32[]{:S(2)}) copy-start(f32[16,1792]{1,0:T(8,128)} %param.9) | copy-start | bytes 344068
  101.4 222.3 %all-gather.5.cloned.1.call-start = ((), (), s32[]{:S(2)}) async-start(), calls=%async_computation.3 | async-start | bytes 1892352 | tf_op jit(solution)/shard_map/all_gather | solution.py:42
  248.8 263.4 %all-gather.3.cloned.1.call-start = ((), (), s32[]{:S(2)}) async-start(), calls=%async_computation.1 | async-start | bytes 8912896 | tf_op jit(solution)/shard_map/all_gather | solution.py:17
Sparse Core Ops, SparseCore 0:
  101.5 145.5 reduce-scatter.1
  251.3 72.4 all-gather.4
  326.0 186.1 all-gather.2
where the time goes:
time: 522 us
  waiting for transfers between devices  409 us (78%)
  blocking collectives  89.5 us (17%)
  between operations  13.8 us (3%)
  matrix products  7.85 us (2%)
    all_gather x1, waiting for transfers between devices, fetch_rows(): whole_basis = lax.all_gather(projector, 'shard', axis=0, tiled=True)  188 us
    reduce_scatter x1, waiting for transfers between devices, on_device(): lax.psum_scatter(lax.dot_general(projected, up_cotangent, (((0,), (0,)),...  146 us
    psum x1, blocking collectives, on_device(): projected = lax.psum(local_proj, 'shard').astype(jnp.bfloat16)  89.5 us
    all_gather x1, waiting for transfers between devices, on_device(): full_step = lax.all_gather(normalized, 'dp', axis=0, tiled=True)  74.2 us
  transfers between devices with their start and end apart: 3, of which 3 were waited for; matrix products, arithmetic and copies ran while one was open for 0% of the time, Pallas kernels for 0%

commit v1 on v0

v1 whole, which is shorter than its diff:
```python
import jax
import jax.numpy as jnp
import numpy as np
from jax import lax
from jax.sharding import Mesh, PartitionSpec as P

STEP = 10

beta_first = 0.9
beta_second = 0.999
epsilon = 1e-08

AXES = ("y", "zh", "core", "x", "zl")
DP = ("y", "zh", "core")
SHARD = ("x", "zl")
bf16 = jnp.bfloat16
f32 = jnp.float32


def dot(a, b):
    return jnp.dot(a, b, preferred_element_type=f32)


def swap_cores(a):
    return lax.ppermute(a, "core", [(0, 1), (1, 0)])


def pick_half(ranks, core):
    rank = lax.broadcasted_iota(jnp.int32, (ranks, ranks // 2), 0)
    at = lax.broadcasted_iota(jnp.int32, (ranks, ranks // 2), 1)
    rows = ranks // 32
    return (rank == (at // rows) * (2 * rows) + core * rows + at % rows).astype(bf16)


def exchange(a, axes, n):
    return lax.all_to_all(a.reshape(n, a.shape[0] // n, a.shape[1]), axes, 0, 0)


def spread(a, axes, n):
    got = lax.all_to_all(jnp.broadcast_to(a, (n, *a.shape)), axes, 0, 0)
    return got.reshape(n * a.shape[0], a.shape[1])


def transposed_pairs():
    ids = np.arange(512).reshape(4, 4, 2, 4, 4)
    return [(int(s), int(d)) for s, d in zip(ids.transpose(3, 4, 2, 0, 1).ravel(), ids.ravel())]


def adam_update(low_grad, first_moment, second_moment):
    first_next = beta_first * first_moment + (1.0 - beta_first) * low_grad
    second_next = beta_second * second_moment + (1.0 - beta_second) * low_grad * low_grad
    first_hat = first_next / (1.0 - beta_first**STEP)
    second_hat = second_next / (1.0 - beta_second**STEP)
    normalized = (first_hat / (jnp.sqrt(second_hat) + epsilon)).astype(bf16)
    return (first_next, second_next, normalized)


def on_device(ffn_input, up_cotangent, projector, first_moment, second_moment):
    tokens, ranks = ffn_input.shape[0], projector.shape[1]
    core = lax.axis_index("core")
    other_input = swap_cores(ffn_input)
    own_half = pick_half(ranks, core)
    half_basis = dot(projector, own_half).astype(bf16)
    local = jnp.concatenate([dot(ffn_input, half_basis), dot(other_input, half_basis)], 0)
    other_cotangent = swap_cores(up_cotangent)
    basis_rows = lax.ppermute(
        lax.dynamic_slice_in_dim(projector, core * 256, 256, 0), AXES, transposed_pairs()
    )
    parts = exchange(local.astype(bf16), SHARD, 16)
    mine = jnp.sum(parts.astype(f32), 0).astype(bf16)
    mine, basis_rows = lax.optimization_barrier((mine, basis_rows))
    projected = spread(mine, SHARD, 16)

    grad = dot(projected[:tokens].T, up_cotangent) + dot(projected[tokens:].T, other_cotangent)
    grad = jnp.sum(exchange(grad.astype(bf16), "y", 4).astype(f32), 0)
    low_grad = jnp.sum(exchange(grad.astype(bf16), "zh", 4).astype(f32), 0)
    first_next, second_next, normalized = adam_update(low_grad, first_moment, second_moment)

    own_step = spread(spread(normalized, "zh", 4), "y", 4)
    other_step = swap_cores(own_step)
    own_rows = dot(basis_rows, own_half).astype(bf16)
    other_rows = dot(basis_rows, pick_half(ranks, 1 - core)).astype(bf16)
    expanded_step = (dot(own_rows, own_step) + dot(other_rows, other_step)).astype(bf16)
    return (expanded_step, first_next, second_next)


def solution(mesh):
    split = Mesh(mesh.devices.reshape(4, 4, 2, 4, 4), AXES)
    in_specs = (
        P(DP, SHARD),
        P(DP, SHARD),
        P(SHARD, None),
        P(DP, SHARD),
        P(DP, SHARD),
    )
    out_specs = (P(DP, SHARD), P(DP, SHARD), P(DP, SHARD))
    return jax.shard_map(
        on_device, mesh=split, in_specs=in_specs, out_specs=out_specs, check_vma=False
    )
```

time: 522 us -> 161 us (0.31)
  waiting for transfers between devices: 409 us -> 35.5 us
  starting transfers between devices: 0.12 us -> 45 us
  blocking collectives: 89.5 us -> 68.3 us
  between operations: 13.8 us -> 0.9 us
    all_gather x2 -> x0, waiting for transfers between devices: 263 us -> none  [the longest x1 188 us: fetch_rows(): whole_basis = lax.all_gather(projector, 'shard', axis=0, tiled=True)]
    reduce_scatter x1 -> x0, waiting for transfers between devices: 146 us -> none  [on_device(): lax.psum_scatter(lax.dot_general(projected, up_cotangent, (((0,), (0,)),...]
    psum x1 -> x0, blocking collectives: 89.5 us -> none  [on_device(): projected = lax.psum(local_proj, 'shard').astype(jnp.bfloat16)]
    all_to_all x0 -> x4, blocking collectives: none -> 68.3 us  [the longest x2 36.1 us: exchange(): return lax.all_to_all(a.reshape(n, a.shape[0] // n, a.shape[1]), axes, 0, 0)]
    all_to_all x0 -> x2, waiting for transfers between devices: none -> 33.7 us  [the longest x1 22.2 us: exchange(): return lax.all_to_all(a.reshape(n, a.shape[0] // n, a.shape[1]), axes, 0, 0)]
    all_to_all x0 -> x2, starting transfers between devices: none -> 25.4 us  [the longest x1 21.7 us: spread(): got = lax.all_to_all(jnp.broadcast_to(a, (n, *a.shape)), axes, 0, 0)]
    ppermute x0 -> x4, starting transfers between devices: none -> 19.6 us  [the longest x3 18.9 us: swap_cores(): return lax.ppermute(a, 'core', [(0, 1), (1, 0)])]
  transfers between devices with their start and end apart: 3 -> 6, of which waited for: 3 -> 4; matrix products, arithmetic and copies ran while one was open for 0% -> 2% of each run, Pallas kernels for 0% -> 0%
where the time goes in v1:
time: 161 us
  blocking collectives  68.3 us (42%)
  starting transfers between devices  45 us (28%)
  waiting for transfers between devices  35.5 us (22%)
  matrix products  7.91 us (5%)
  local copies, waits for them, and re-layouts  2.02 us (1%)
    all_to_all x2, blocking collectives, exchange(): return lax.all_to_all(a.reshape(n, a.shape[0] // n, a.shape[1]), axes, 0, 0)  36.1 us
    all_to_all x2, blocking collectives, spread(): got = lax.all_to_all(jnp.broadcast_to(a, (n, *a.shape)), axes, 0, 0)  32.2 us
    all_to_all x1, waiting for transfers between devices, exchange(): return lax.all_to_all(a.reshape(n, a.shape[0] // n, a.shape[1]), axes, 0, 0)  22.2 us
    all_to_all x1, starting transfers between devices, spread(): got = lax.all_to_all(jnp.broadcast_to(a, (n, *a.shape)), axes, 0, 0)  21.7 us
    ppermute x3, starting transfers between devices, swap_cores(): return lax.ppermute(a, 'core', [(0, 1), (1, 0)])  18.9 us
    all_to_all x1, waiting for transfers between devices, spread(): got = lax.all_to_all(jnp.broadcast_to(a, (n, *a.shape)), axes, 0, 0)  11.4 us
    dot_general x7, matrix products, dot(): return jnp.dot(a, b, preferred_element_type=f32)  7.91 us
    all_to_all x1, starting transfers between devices, exchange(): return lax.all_to_all(a.reshape(n, a.shape[0] // n, a.shape[1]), axes, 0, 0)  3.71 us
  transfers between devices with their start and end apart: 6, of which 4 were waited for; matrix products, arithmetic and copies ran while one was open for 2% of the time, Pallas kernels for 0%

profile of v1, /device:TPU:1, one launch (start us, length us, event | category | flops | bytes accessed | tf_op | source)
XLA Modules:
  0.0 160.8 jit_solution(8732631813986090208)
XLA Ops:
  0.6 0.0 copy-start
  0.6 0.0 copy-start.2
  0.7 8.9 %collective-permute-start = (bf16[512,512]{1,0:T(8,128)(2,1)}, bf16[512,512]{1,0:T(8,128)(2,1)S(1)}, u32[]{:S(2)}, u32[]{:S(2)}) collective-permute-start(bf16[512,512]{1,0:T(8,128)(2,1)} %param.5), channel_id=1, source_target_pairs={{0,16},{16,0},{1,17},{17,1},{2,18},{18,2},{3,19},{19,3},{4,20},{20... | collective-permute-start | bytes 1572872 | tf_op jit(solution)/shard_map/ppermute | solution.py:25
  9.6 0.0 copy-start.5
  9.6 0.0 copy-start.6
  9.6 0.0 copy-done
  9.7 0.4 convolution_convert_fusion
  10.0 0.0 copy-done.2
  10.0 0.3 fusion.2
  10.4 0.9 collective-permute-done
  11.3 0.3 fusion.3
  11.6 0.0 copy-done.5
  11.7 0.0 copy-done.6
  11.7 0.1 pad_maximum_fusion
  11.7 1.0 copy.9
  12.7 0.0 copy-start.1
  12.7 3.7 %all-to-all-start = ((bf16[16,64,256]{2,1,0:T(8,128)(2,1)}), bf16[16,64,256]{2,1,0:T(8,128)(2,1)S(1)}, u32[]{:S(2)}, u32[]{:S(2)}) async-start(bf16[16,64,256]{2,1,0:T(8,128)(2,1)} %bitcast.2), calls=%async_computation | async-start | bytes 1048576 | tf_op jit(solution)/shard_map/all_to_all | solution.py:36
  16.5 0.7 collective-permute-start.1
  17.2 22.2 %all-to-all-done = bf16[16,64,256]{2,1,0:T(8,128)(2,1)S(1)} async-done(((bf16[16,64,256]{2,1,0:T(8,128)(2,1)}), bf16[16,64,256]{2,1,0:T(8,128)(2,1)S(1)}, u32[]{:S(2)}, u32[]{:S(2)}) %all-to-all-start) | async-done | bytes 524320 | tf_op jit(solution)/shard_map/all_to_all | solution.py:36
  39.4 0.1 reduce_sum.33
  39.5 0.0 collective-permute-done.1
  39.5 0.8 broadcast_in_dim.9
  40.3 21.7 %all-to-all-start.1 = ((bf16[16,64,256]{2,1,0:T(8,128)(2,1)}), bf16[16,64,256]{2,1,0:T(8,128)(2,1)S(1)}, u32[]{:S(2)}, u32[]{:S(2)}) async-start(bf16[16,64,256]{2,1,0:T(8,128)(2,1)} %broadcast_in_dim.9), calls=%async_computation.1 | async-start | bytes 1048576 | tf_op jit(solution)/shard_map/all_to_all | solution.py:40
  62.1 0.0 copy-done.1
  62.1 4.1 %collective-permute-start.2 = (bf16[512,1792]{1,0:T(8,128)(2,1)S(1)}, bf16[512,1792]{1,0:T(8,128)(2,1)}, u32[]{:S(2)}, u32[]{:S(2)}) collective-permute-start(bf16[512,1792]{1,0:T(8,128)(2,1)S(1)} %copy-done.1), channel_id=1, source_target_pairs={{0,16},{16,0},{1,17},{17,1},{2,18},{18,2},{3,19},{19,3},{4,20},{20... | collective-permute-start | bytes 5505032 | tf_op jit(solution)/shard_map/ppermute | solution.py:25
  66.1 11.4 %all-to-all-done.1 = bf16[16,64,256]{2,1,0:T(8,128)(2,1)S(1)} async-done(((bf16[16,64,256]{2,1,0:T(8,128)(2,1)}), bf16[16,64,256]{2,1,0:T(8,128)(2,1)S(1)}, u32[]{:S(2)}, u32[]{:S(2)}) %all-to-all-start.1) | async-done | bytes 524320 | tf_op jit(solution)/shard_map/all_to_all | solution.py:40
  77.6 0.7 fusion.36
  78.3 0.0 collective-permute-done.2
  78.3 2.2 %fusion.1 = bf16[256,1792]{1,0:T(8,128)(2,1)S(1)} fusion(f32[256,1792]{1,0:T(8,128)S(1)} %fusion.36, bf16[512,256]{1,0:T(8,128)(2,1)S(1)} %bitcast.27, bf16[512,1792]{1,0:T(8,128)(2,1)} %collective-permute-done.2), kind=kOutput, calls=%fused_computation.3 | convolution fusion | flops 470679552 | bytes 4849664 | tf_op jit(solution)/shard_map/dot_general | solution.py:21
  80.4 0.0 copy-start.3
  80.4 0.0 copy-start.4
  80.5 13.9 %all_to_all.30 = bf16[4,64,1792]{2,1,0:T(8,128)(2,1)S(1)} all-to-all(bf16[4,64,1792]{2,1,0:T(8,128)(2,1)S(1)} %bitcast.24), channel_id=1, replica_groups=mesh['y'=4,'zh'=4,'core'=2,'x'=4,'zl'=4] {'y'}, dimensions={0} | all-to-all | bytes 1835008 | tf_op jit(solution)/shard_map/all_to_all | solution.py:36
  94.3 0.2 reduce_sum.34
  94.5 22.2 %all_to_all.31 = bf16[4,16,1792]{2,1,0:T(8,128)(2,1)S(1)} all-to-all(bf16[4,16,1792]{2,1,0:T(8,128)(2,1)S(1)} %bitcast.29), channel_id=1, replica_groups=mesh['y'=4,'zh'=4,'core'=2,'x'=4,'zl'=4] {'zh'}, dimensions={0} | all-to-all | bytes 458752 | tf_op jit(solution)/shard_map/all_to_all | solution.py:36
  116.7 0.0 copy-done.3
  116.8 0.0 copy-done.4
  116.8 0.8 divide_convert_fusion
  117.5 19.2 %all_to_all.32 = bf16[4,16,1792]{2,1,0:T(8,128)(2,1)S(1)} all-to-all(bf16[4,16,1792]{2,1,0:T(8,128)(2,1)S(1)} %broadcast_in_dim.10), channel_id=1, replica_groups=mesh['y'=4,'zh'=4,'core'=2,'x'=4,'zl'=4] {'zh'}, dimensions={0} | all-to-all | bytes 458752 | tf_op jit(solution)/shard_map/all_to_all | solution.py:40
  136.8 0.1 broadcast_in_dim.11
  136.8 13.0 %all_to_all.33 = bf16[4,64,1792]{2,1,0:T(8,128)(2,1)S(1)} all-to-all(bf16[4,64,1792]{2,1,0:T(8,128)(2,1)S(1)} %broadcast_in_dim.11), channel_id=1, replica_groups=mesh['y'=4,'zh'=4,'core'=2,'x'=4,'zl'=4] {'y'}, dimensions={0} | all-to-all | bytes 1835008 | tf_op jit(solution)/shard_map/all_to_all | solution.py:40
  149.8 6.0 %collective-permute-start.3 = (bf16[256,1792]{1,0:T(8,128)(2,1)S(1)}, bf16[256,1792]{1,0:T(8,128)(2,1)}, u32[]{:S(2)}, u32[]{:S(2)}) collective-permute-start(bf16[256,1792]{1,0:T(8,128)(2,1)S(1)} %bitcast.25), channel_id=1, source_target_pairs={{0,16},{16,0},{1,17},{17,1},{2,18},{18,2},{3,19},{19,3},{4,20},{20... | collective-permute-start | bytes 2752520 | tf_op jit(solution)/shard_map/ppermute | solution.py:25
  155.8 1.3 fusion.4
  157.1 0.9 collective-permute-done.3
  158.0 2.8 %fusion = bf16[256,1792]{1,0:T(8,128)(2,1)} fusion(f32[256,1792]{1,0:T(8,128)S(1)} %fusion.4, bf16[256,1792]{1,0:T(8,128)(2,1)} %collective-permute-done.3, bf16[256,512]{1,0:T(8,128)(2,1)S(1)} %collective-permute-done.1, s32[]{:T(128)S(6)} %mul.54, s32[256]{0:T(256)S(1)} %get-tuple-element.13, s32[256]{0:T(256)S(1)} %get-tuple-element.16, ...), kind=kOutput, calls=%fused_computation.2 | convolution fusion | flops 303759360 | bytes 3936772 | tf_op jit(solution)/shard_map/dot_general | solution.py:21
  (7 shorter events, 0.1 us)
Async XLA Ops:
  0.6 9.0 %copy-start = (bf16[512,512]{1,0:T(8,128)(2,1)S(1)}, bf16[512,512]{1,0:T(8,128)(2,1)}, u32[]{:S(2)}) copy-start(bf16[512,512]{1,0:T(8,128)(2,1)} %param.7) | copy-start | bytes 1572868
  0.6 9.4 %copy-start.2 = (bf16[512,512]{1,0:T(8,128)(2,1)S(1)}, bf16[512,512]{1,0:T(8,128)(2,1)}, u32[]{:S(2)}) copy-start(bf16[512,512]{1,0:T(8,128)(2,1)} %param.5) | copy-start | bytes 1572868
  0.7 10.7 %collective-permute-start = (bf16[512,512]{1,0:T(8,128)(2,1)}, bf16[512,512]{1,0:T(8,128)(2,1)S(1)}, u32[]{:S(2)}, u32[]{:S(2)}) collective-permute-start(bf16[512,512]{1,0:T(8,128)(2,1)} %param.5), channel_id=1, source_target_pairs={{0,16},{16,0},{1,17},{17,1},{2,18},{18,2},{3,19},{19,3},{4,20},{20... | collective-permute-start | bytes 1572872 | tf_op jit(solution)/shard_map/ppermute | solution.py:25
  9.6 2.0 %copy-start.5 = (pred[256]{0:T(512)(128)(4,1)}, pred[256]{0:T(512)(128)(4,1)S(1)}, u32[]{:S(2)}) copy-start(pred[256]{0:T(512)(128)(4,1)S(1)} %get-tuple-element.14) | copy-start | bytes 772
  9.6 2.0 %copy-start.6 = (pred[256]{0:T(512)(128)(4,1)}, pred[256]{0:T(512)(128)(4,1)S(1)}, u32[]{:S(2)}) copy-start(pred[256]{0:T(512)(128)(4,1)S(1)} %get-tuple-element.15) | copy-start | bytes 772
  12.7 49.3 %copy-start.1 = (bf16[512,1792]{1,0:T(8,128)(2,1)S(1)}, bf16[512,1792]{1,0:T(8,128)(2,1)}, u32[]{:S(2)}) copy-start(bf16[512,1792]{1,0:T(8,128)(2,1)} %param.6) | copy-start | bytes 5505028
  12.7 26.7 %all-to-all-start = ((bf16[16,64,256]{2,1,0:T(8,128)(2,1)}), bf16[16,64,256]{2,1,0:T(8,128)(2,1)S(1)}, u32[]{:S(2)}, u32[]{:S(2)}) async-start(bf16[16,64,256]{2,1,0:T(8,128)(2,1)} %bitcast.2), calls=%async_computation | async-start | bytes 1048576 | tf_op jit(solution)/shard_map/all_to_all | solution.py:36
  16.5 23.0 %collective-permute-start.1 = (bf16[256,512]{1,0:T(8,128)(2,1)S(1)}, bf16[256,512]{1,0:T(8,128)(2,1)S(1)}, u32[]{:S(2)}, u32[]{:S(2)}) collective-permute-start(bf16[256,512]{1,0:T(8,128)(2,1)S(1)} %constant_dynamic-slice_fusion), channel_id=1, source_target_pairs={{0,0},{32,1},{64,2},{96,3},{128,4},{160,5},{192,6},{224,7},{256,8}... | collective-permute-start | bytes 786440 | tf_op jit(solution)/shard_map/ppermute | solution.py:66
  40.3 37.2 %all-to-all-start.1 = ((bf16[16,64,256]{2,1,0:T(8,128)(2,1)}), bf16[16,64,256]{2,1,0:T(8,128)(2,1)S(1)}, u32[]{:S(2)}, u32[]{:S(2)}) async-start(bf16[16,64,256]{2,1,0:T(8,128)(2,1)} %broadcast_in_dim.9), calls=%async_computation.1 | async-start | bytes 1048576 | tf_op jit(solution)/shard_map/all_to_all | solution.py:40
  62.1 16.2 %collective-permute-start.2 = (bf16[512,1792]{1,0:T(8,128)(2,1)S(1)}, bf16[512,1792]{1,0:T(8,128)(2,1)}, u32[]{:S(2)}, u32[]{:S(2)}) collective-permute-start(bf16[512,1792]{1,0:T(8,128)(2,1)S(1)} %copy-done.1), channel_id=1, source_target_pairs={{0,16},{16,0},{1,17},{17,1},{2,18},{18,2},{3,19},{19,3},{4,20},{20... | collective-permute-start | bytes 5505032 | tf_op jit(solution)/shard_map/ppermute | solution.py:25
  80.4 36.3 %copy-start.3 = (f32[16,1792]{1,0:T(8,128)S(1)}, f32[16,1792]{1,0:T(8,128)}, u32[]{:S(2)}) copy-start(f32[16,1792]{1,0:T(8,128)} %param.8) | copy-start | bytes 344068
  80.4 36.3 %copy-start.4 = (f32[16,1792]{1,0:T(8,128)S(1)}, f32[16,1792]{1,0:T(8,128)}, u32[]{:S(2)}) copy-start(f32[16,1792]{1,0:T(8,128)} %param.9) | copy-start | bytes 344068
  149.8 8.2 %collective-permute-start.3 = (bf16[256,1792]{1,0:T(8,128)(2,1)S(1)}, bf16[256,1792]{1,0:T(8,128)(2,1)}, u32[]{:S(2)}, u32[]{:S(2)}) collective-permute-start(bf16[256,1792]{1,0:T(8,128)(2,1)S(1)} %bitcast.25), channel_id=1, source_target_pairs={{0,16},{16,0},{1,17},{17,1},{2,18},{18,2},{3,19},{19,3},{4,20},{20... | collective-permute-start | bytes 2752520 | tf_op jit(solution)/shard_map/ppermute | solution.py:25

commit v2 on v1

--- a/solution.py
+++ b/solution.py
@@ -16,9 +16,15 @@
 bf16 = jnp.bfloat16
 f32 = jnp.float32
 
+NEAR = ((0, 3, 1, 2), (2, 0, 3, 1), (3, 0, 1, 2), (2, 3, 0, 1))
+
 
 def dot(a, b):
     return jnp.dot(a, b, preferred_element_type=f32)
+
+
+def dot_rows(a, b):
+    return lax.dot_general(a, b, (((0,), (0,)), ((), ())), preferred_element_type=f32)
 
 
 def swap_cores(a):
@@ -32,8 +38,19 @@
     return (rank == (at // rows) * (2 * rows) + core * rows + at % rows).astype(bf16)
 
 
+def pick_all(ranks):
+    return jnp.concatenate([pick_half(ranks, 0), pick_half(ranks, 1)], 1)
+
+
 def exchange(a, axes, n):
     return lax.all_to_all(a.reshape(n, a.shape[0] // n, a.shape[1]), axes, 0, 0)
+
+
+def add_up(parts):
+    total = parts[0].astype(f32)
+    for i in range(1, parts.shape[0]):
+        total = total + parts[i].astype(f32)
+    return total
 
 
 def spread(a, axes, n):
@@ -41,9 +58,22 @@
     return got.reshape(n * a.shape[0], a.shape[1])
 
 
-def transposed_pairs():
+STEPS = [('x', 2), ('z', 2), ('z', 1), ('x', 1)]
+
+
+def hand_on(a, step):
     ids = np.arange(512).reshape(4, 4, 2, 4, 4)
-    return [(int(s), int(d)) for s, d in zip(ids.transpose(3, 4, 2, 0, 1).ravel(), ids.ravel())]
+    has = [(0, 0)]
+    for axis, bit in STEPS[: STEPS.index(step)]:
+        has += [(dx ^ bit, dz) if axis == "x" else (dx, dz ^ bit) for dx, dz in has]
+    pairs = []
+    for y, zh, c in np.ndindex(4, 4, 2):
+        for dx, dz in has:
+            to = (dx ^ step[1], dz) if step[0] == "x" else (dx, dz ^ step[1])
+            pairs.append(
+                (int(ids[y, zh, c, y ^ dx, zh ^ dz]), int(ids[y, zh, c, y ^ to[0], zh ^ to[1]]))
+            )
+    return lax.ppermute(a, AXES, pairs)
 
 
 def adam_update(low_grad, first_moment, second_moment):
@@ -57,29 +87,49 @@
 
 def on_device(ffn_input, up_cotangent, projector, first_moment, second_moment):
     tokens, ranks = ffn_input.shape[0], projector.shape[1]
+    half = ranks // 2
     core = lax.axis_index("core")
-    other_input = swap_cores(ffn_input)
-    own_half = pick_half(ranks, core)
-    half_basis = dot(projector, own_half).astype(bf16)
-    local = jnp.concatenate([dot(ffn_input, half_basis), dot(other_input, half_basis)], 0)
     other_cotangent = swap_cores(up_cotangent)
-    basis_rows = lax.ppermute(
-        lax.dynamic_slice_in_dim(projector, core * 256, 256, 0), AXES, transposed_pairs()
+    ordered = lax.optimization_barrier(dot(projector, pick_all(ranks)).astype(bf16))
+    rows = ordered.shape[0] // 2
+    has_rows = (lax.axis_index("x") == lax.axis_index("y")) & (
+        lax.axis_index("zl") == lax.axis_index("zh")
     )
-    parts = exchange(local.astype(bf16), SHARD, 16)
-    mine = jnp.sum(parts.astype(f32), 0).astype(bf16)
-    mine, basis_rows = lax.optimization_barrier((mine, basis_rows))
-    projected = spread(mine, SHARD, 16)
-
-    grad = dot(projected[:tokens].T, up_cotangent) + dot(projected[tokens:].T, other_cotangent)
-    grad = jnp.sum(exchange(grad.astype(bf16), "y", 4).astype(f32), 0)
-    low_grad = jnp.sum(exchange(grad.astype(bf16), "zh", 4).astype(f32), 0)
+    basis = lax.dynamic_slice_in_dim(ordered, core * rows, rows, 0)
+    basis = jnp.where(has_rows, basis, 0)
+    local = dot(ffn_input, ordered).astype(bf16)
+    local, basis = lax.optimization_barrier((local, basis))
+    came = hand_on(basis, ('x', 2))
+    parts, came = lax.optimization_barrier((exchange(local, SHARD, 16), came))
+    basis = basis + came
+    mine = add_up(parts).astype(bf16)
+    halves = jnp.stack([mine[:, :half], mine[:, half:]], 0)
+    halves = jnp.broadcast_to(halves[:, None], (2, 16, *halves.shape[1:]))
+    halves = halves.reshape(32, *halves.shape[2:])
+    got = lax.all_to_all(halves, ("core", *SHARD), 0, 0)
+    projected = got.reshape(2, tokens, half)
+    own = lax.dynamic_index_in_dim(projected, core, 0, False)
+    other = lax.dynamic_index_in_dim(projected, 1 - core, 0, False)
+    grad = dot_rows(own, up_cotangent) + dot_rows(other, other_cotangent)
+    grad = grad.astype(bf16)
+    grad, basis = lax.optimization_barrier((grad, basis))
+    basis = basis + hand_on(basis, ('z', 2))
+    came = hand_on(basis, ('z', 1))
+    grad, came = lax.optimization_barrier((exchange(grad, "y", 4), came))
+    basis = basis + came
+    grad = add_up(grad).astype(bf16)
+    grad, basis = lax.optimization_barrier((grad, basis))
+    came = hand_on(basis, ('x', 1))
+    grad, came = lax.optimization_barrier((exchange(grad, "zh", 4), came))
+    basis = basis + came
+    low_grad = add_up(grad)
     first_next, second_next, normalized = adam_update(low_grad, first_moment, second_moment)
-
-    own_step = spread(spread(normalized, "zh", 4), "y", 4)
+    quarter_step = spread(normalized, "zh", 4)
+    own_step = spread(quarter_step, "y", 4)
+    low_rows, high_rows = basis[:, :half], basis[:, half:]
     other_step = swap_cores(own_step)
-    own_rows = dot(basis_rows, own_half).astype(bf16)
-    other_rows = dot(basis_rows, pick_half(ranks, 1 - core)).astype(bf16)
+    own_rows = jnp.where(core == 0, low_rows, high_rows)
+    other_rows = jnp.where(core == 0, high_rows, low_rows)
     expanded_step = (dot(own_rows, own_step) + dot(other_rows, other_step)).astype(bf16)
     return (expanded_step, first_next, second_next)
 

time: 161 us -> 145 us (0.901)
  blocking collectives: 68.3 us -> 30.2 us
  starting transfers between devices: 45 us -> 55.8 us
  waiting for transfers between devices: 35.5 us -> 45.4 us
  other arithmetic: 1.09 us -> 3.1 us
    all_to_all x2 -> x0, blocking collectives: 36.1 us -> none  [exchange(): return lax.all_to_all(a.reshape(n, a.shape[0] // n, a.shape[1]), axes, 0, 0)]
    all_to_all x1 -> x3, starting transfers between devices: 3.71 us -> 28 us  [exchange(): return lax.all_to_all(a.reshape(n, a.shape[0] // n, a.shape[1]), axes, 0, 0)]
    ppermute x1 -> x4, waiting for transfers between devices: 0.01 us -> 16.7 us  [hand_on(): return lax.ppermute(a, AXES, pairs)]
    all_to_all x1, starting transfers between devices: 21.7 us -> 5.4 us  [on_device(): got = lax.all_to_all(halves, ('core', *SHARD), 0, 0)]
    ppermute x1 -> x4, starting transfers between devices: 0.68 us -> 11.6 us  [hand_on(): return lax.ppermute(a, AXES, pairs)]
    ppermute x3 -> x2, starting transfers between devices: 18.9 us -> 10.8 us  [swap_cores(): return lax.ppermute(a, 'core', [(0, 1), (1, 0)])]
    all_to_all x1 -> x3, waiting for transfers between devices: 22.2 us -> 15.1 us  [exchange(): return lax.all_to_all(a.reshape(n, a.shape[0] // n, a.shape[1]), axes, 0, 0)]
    dot_general x7 -> x4, matrix products: 7.91 us -> 2.78 us  [dot(): return jnp.dot(a, b, preferred_element_type=f32)]
  transfers between devices with their start and end apart: 6 -> 10, of which waited for: 4 -> 8; matrix products, arithmetic and copies ran while one was open for 2% -> 2% of each run, Pallas kernels for 0% -> 0%
where the time goes in v2:
time: 145 us
  starting transfers between devices  55.8 us (38%)
  waiting for transfers between devices  45.4 us (31%)
  blocking collectives  30.2 us (21%)
  matrix products  6.55 us (5%)
  other arithmetic  3.1 us (2%)
  local copies, waits for them, and re-layouts  2.77 us (2%)
    all_to_all x2, blocking collectives, spread(): got = lax.all_to_all(jnp.broadcast_to(a, (n, *a.shape)), axes, 0, 0)  30.2 us
    all_to_all x3, starting transfers between devices, exchange(): return lax.all_to_all(a.reshape(n, a.shape[0] // n, a.shape[1]), axes, 0, 0)  28 us
    ppermute x4, waiting for transfers between devices, hand_on(): return lax.ppermute(a, AXES, pairs)  16.7 us
    all_to_all x3, waiting for transfers between devices, exchange(): return lax.all_to_all(a.reshape(n, a.shape[0] // n, a.shape[1]), axes, 0, 0)  15.1 us
    all_to_all x1, waiting for transfers between devices, on_device(): got = lax.all_to_all(halves, ('core', *SHARD), 0, 0)  12.1 us
    ppermute x4, starting transfers between devices, hand_on(): return lax.ppermute(a, AXES, pairs)  11.6 us
    ppermute x2, starting transfers between devices, swap_cores(): return lax.ppermute(a, 'core', [(0, 1), (1, 0)])  10.8 us
    all_to_all x1, starting transfers between devices, on_device(): got = lax.all_to_all(halves, ('core', *SHARD), 0, 0)  5.4 us
  transfers between devices with their start and end apart: 10, of which 8 were waited for; matrix products, arithmetic and copies ran while one was open for 2% of the time, Pallas kernels for 0%

profile of v2, /device:TPU:1, one launch (start us, length us, event | category | flops | bytes accessed | tf_op | source)
XLA Modules:
  0.0 144.7 jit_solution(4019376443793079762)
XLA Ops:
  0.6 0.0 copy-start
  0.6 0.0 copy-start.2
  0.7 0.2 fusion.4
  0.9 0.8 copy-done
  1.7 0.5 fusion.3
  2.2 0.0 copy-done.2
  2.2 0.5 fusion.2
  2.7 0.1 dynamic-slice_select_fusion
  2.7 1.0 copy.24
  3.7 0.0 copy-start.1
  3.7 9.1 %all-to-all-start = ((bf16[16,32,512]{2,1,0:T(8,128)(2,1)}), bf16[16,32,512]{2,1,0:T(8,128)(2,1)S(1)}, u32[]{:S(2)}, u32[]{:S(2)}) async-start(bf16[16,32,512]{2,1,0:T(8,128)(2,1)} %bitcast.2), calls=%async_computation | async-start | bytes 1048576 | tf_op jit(solution)/shard_map/all_to_all | solution.py:46
  12.9 5.5 %collective-permute-start = (bf16[256,512]{0,1:T(8,128)(2,1)S(1)}, bf16[256,512]{0,1:T(8,128)(2,1)}, u32[]{:S(2)}, u32[]{:S(2)}) collective-permute-start(bf16[256,512]{0,1:T(8,128)(2,1)S(1)} %dynamic-slice_select_fusion), channel_id=1, source_target_pairs={{0,8},{16,24},{33,41},{49,57},{66,74},{82,90},{99,107},{115,123},{... | collective-permute-start | bytes 786440 | tf_op jit(solution)/shard_map/ppermute | solution.py:76
  18.4 5.4 %collective-permute-done = bf16[256,512]{0,1:T(8,128)(2,1)} collective-permute-done((bf16[256,512]{0,1:T(8,128)(2,1)S(1)}, bf16[256,512]{0,1:T(8,128)(2,1)}, u32[]{:S(2)}, u32[]{:S(2)}) %collective-permute-start) | collective-permute-done | bytes 262176 | tf_op jit(solution)/shard_map/ppermute | solution.py:76
  23.7 4.9 %all-to-all-done = bf16[16,32,512]{2,1,0:T(8,128)(2,1)S(1)} async-done(((bf16[16,32,512]{2,1,0:T(8,128)(2,1)}), bf16[16,32,512]{2,1,0:T(8,128)(2,1)S(1)}, u32[]{:S(2)}, u32[]{:S(2)}) %all-to-all-start) | async-done | bytes 524320 | tf_op jit(solution)/shard_map/all_to_all | solution.py:46
  28.6 0.1 fusion.23
  28.7 0.9 broadcast_in_dim.17
  29.5 5.4 %all-to-all-start.1 = ((bf16[32,32,256]{2,1,0:T(8,128)(2,1)}), bf16[32,32,256]{2,1,0:T(8,128)(2,1)S(1)}, u32[]{:S(2)}, u32[]{:S(2)}) async-start(bf16[32,32,256]{2,1,0:T(8,128)(2,1)} %bitcast.7), calls=%async_computation.1 | async-start | bytes 1048576 | tf_op jit(solution)/shard_map/all_to_all | solution.py:109
  35.0 0.0 copy-done.1
  35.0 2.2 %collective-permute-start.1 = (bf16[512,1792]{1,0:T(8,128)(2,1)S(1)}, bf16[512,1792]{1,0:T(8,128)(2,1)}, u32[]{:S(2)}, u32[]{:S(2)}) collective-permute-start(bf16[512,1792]{1,0:T(8,128)(2,1)S(1)} %copy-done.1), channel_id=1, source_target_pairs={{0,16},{16,0},{1,17},{17,1},{2,18},{18,2},{3,19},{19,3},{4,20},{20... | collective-permute-start | bytes 5505032 | tf_op jit(solution)/shard_map/ppermute | solution.py:31
  37.1 1.0 add.166
  38.1 12.1 %all-to-all-done.1 = bf16[32,32,256]{2,1,0:T(8,128)(2,1)S(1)} async-done(((bf16[32,32,256]{2,1,0:T(8,128)(2,1)}), bf16[32,32,256]{2,1,0:T(8,128)(2,1)S(1)}, u32[]{:S(2)}, u32[]{:S(2)}) %all-to-all-start.1) | async-done | bytes 524320 | tf_op jit(solution)/shard_map/all_to_all | solution.py:109
  50.2 0.7 fusion.7
  50.9 0.0 collective-permute-done.1
  50.9 3.1 %fusion.1 = bf16[256,1792]{1,0:T(8,128)(2,1)} fusion(f32[256,1792]{1,0:T(8,128)S(1)} %fusion.7, bf16[512,1792]{1,0:T(8,128)(2,1)} %collective-permute-done.1, bf16[2,512,256]{2,1,0:T(8,128)(2,1)S(1)} %bitcast.45, s32[]{:T(128)S(6)} %select_n.56), kind=kOutput, calls=%fused_computation.3 | convolution fusion | flops 470679552 | bytes 4849668 | tf_op jit(solution)/shard_map/dot_general | solution.py:27
  54.0 4.2 %all-to-all-start.2 = ((bf16[4,64,1792]{2,1,0:T(8,128)(2,1)}), bf16[4,64,1792]{2,1,0:T(8,128)(2,1)S(1)}, u32[]{:S(2)}, u32[]{:S(2)}) async-start(bf16[4,64,1792]{2,1,0:T(8,128)(2,1)} %bitcast.11), calls=%async_computation.2 | async-start | bytes 1835008 | tf_op jit(solution)/shard_map/all_to_all | solution.py:46
  58.2 3.5 %collective-permute-start.2 = (bf16[256,512]{0,1:T(8,128)(2,1)S(1)}, bf16[256,512]{0,1:T(8,128)(2,1)S(1)}, u32[]{:S(2)}, u32[]{:S(2)}) collective-permute-start(bf16[256,512]{0,1:T(8,128)(2,1)S(1)} %add.166), channel_id=1, source_target_pairs={{0,2},{8,10},{16,18},{24,26},{33,35},{41,43},{49,51},{57,59},{66,6... | collective-permute-start | bytes 786440 | tf_op jit(solution)/shard_map/ppermute | solution.py:76
  61.7 4.3 %collective-permute-done.2 = bf16[256,512]{0,1:T(8,128)(2,1)S(1)} collective-permute-done((bf16[256,512]{0,1:T(8,128)(2,1)S(1)}, bf16[256,512]{0,1:T(8,128)(2,1)S(1)}, u32[]{:S(2)}, u32[]{:S(2)}) %collective-permute-start.2) | collective-permute-done | bytes 262176 | tf_op jit(solution)/shard_map/ppermute | solution.py:76
  66.0 0.1 add.167
  66.1 1.3 collective-permute-start.3
  67.4 3.7 %collective-permute-done.3 = bf16[256,512]{0,1:T(8,128)(2,1)S(1)} collective-permute-done((bf16[256,512]{0,1:T(8,128)(2,1)S(1)}, bf16[256,512]{0,1:T(8,128)(2,1)S(1)}, u32[]{:S(2)}, u32[]{:S(2)}) %collective-permute-start.3) | collective-permute-done | bytes 262176 | tf_op jit(solution)/shard_map/ppermute | solution.py:76
  71.1 0.0 all-to-all-done.2
  71.1 0.8 fusion.11
  71.9 0.1 add.172
  72.0 14.7 %all-to-all-start.3 = ((bf16[4,16,1792]{2,1,0:T(8,128)(2,1)}), bf16[4,16,1792]{2,1,0:T(8,128)(2,1)S(1)}, u32[]{:S(2)}, u32[]{:S(2)}) async-start(bf16[4,16,1792]{2,1,0:T(8,128)(2,1)} %bitcast.13), calls=%async_computation.3 | async-start | bytes 458752 | tf_op jit(solution)/shard_map/all_to_all | solution.py:46
  86.7 1.3 collective-permute-start.4
  88.0 3.3 %collective-permute-done.4 = bf16[256,512]{0,1:T(8,128)(2,1)S(1)} collective-permute-done((bf16[256,512]{0,1:T(8,128)(2,1)S(1)}, bf16[256,512]{0,1:T(8,128)(2,1)S(1)}, u32[]{:S(2)}, u32[]{:S(2)}) %collective-permute-start.4) | collective-permute-done | bytes 262176 | tf_op jit(solution)/shard_map/ppermute | solution.py:76
  91.3 10.3 %all-to-all-done.3 = bf16[4,16,1792]{2,1,0:T(8,128)(2,1)S(1)} async-done(((bf16[4,16,1792]{2,1,0:T(8,128)(2,1)}), bf16[4,16,1792]{2,1,0:T(8,128)(2,1)S(1)}, u32[]{:S(2)}, u32[]{:S(2)}) %all-to-all-start.3) | async-done | bytes 229408 | tf_op jit(solution)/shard_map/all_to_all | solution.py:46
  101.5 0.0 copy-done.3
  101.5 0.0 copy-done.4
  101.5 0.8 divide_convert_fusion
  102.3 18.5 %all_to_all.30 = bf16[4,16,1792]{2,1,0:T(8,128)(2,1)S(1)} all-to-all(bf16[4,16,1792]{2,1,0:T(8,128)(2,1)S(1)} %broadcast_in_dim.18), channel_id=1, replica_groups=mesh['y'=4,'zh'=4,'core'=2,'x'=4,'zl'=4] {'zh'}, dimensions={0} | all-to-all | bytes 458752 | tf_op jit(solution)/shard_map/all_to_all | solution.py:57
  120.9 0.1 broadcast_in_dim.19
  120.9 11.7 %all_to_all.31 = bf16[4,64,1792]{2,1,0:T(8,128)(2,1)S(1)} all-to-all(bf16[4,64,1792]{2,1,0:T(8,128)(2,1)S(1)} %broadcast_in_dim.19), channel_id=1, replica_groups=mesh['y'=4,'zh'=4,'core'=2,'x'=4,'zl'=4] {'y'}, dimensions={0} | all-to-all | bytes 1835008 | tf_op jit(solution)/shard_map/all_to_all | solution.py:57
  132.6 8.6 %collective-permute-start.5 = (bf16[256,1792]{1,0:T(8,128)(2,1)S(1)}, bf16[256,1792]{1,0:T(8,128)(2,1)S(1)}, u32[]{:S(2)}, u32[]{:S(2)}) collective-permute-start(bf16[256,1792]{1,0:T(8,128)(2,1)S(1)} %bitcast.42), channel_id=1, source_target_pairs={{0,16},{16,0},{1,17},{17,1},{2,18},{18,2},{3,19},{19,3},{4,20},{20... | collective-permute-start | bytes 2752520 | tf_op jit(solution)/shard_map/ppermute | solution.py:31
  141.2 0.1 add.173
  141.3 0.5 fusion.13
  141.7 1.5 %collective-permute-done.5 = bf16[256,1792]{1,0:T(8,128)(2,1)S(1)} collective-permute-done((bf16[256,1792]{1,0:T(8,128)(2,1)S(1)}, bf16[256,1792]{1,0:T(8,128)(2,1)S(1)}, u32[]{:S(2)}, u32[]{:S(2)}) %collective-permute-start.5) | collective-permute-done | bytes 917536 | tf_op jit(solution)/shard_map/ppermute | solution.py:31
  143.3 1.4 fusion
  (8 shorter events, 0.0 us)
Async XLA Ops:
  0.6 1.0 copy-start
  0.6 1.5 %copy-start.2 = (bf16[512,512]{1,0:T(8,128)(2,1)S(1)}, bf16[512,512]{1,0:T(8,128)(2,1)}, u32[]{:S(2)}) copy-start(bf16[512,512]{1,0:T(8,128)(2,1)} %param.5) | copy-start | bytes 1572868
  3.7 31.2 %copy-start.1 = (bf16[512,1792]{1,0:T(8,128)(2,1)S(1)}, bf16[512,1792]{1,0:T(8,128)(2,1)}, u32[]{:S(2)}) copy-start(bf16[512,1792]{1,0:T(8,128)(2,1)} %param.6) | copy-start | bytes 5505028
  3.7 24.9 %all-to-all-start = ((bf16[16,32,512]{2,1,0:T(8,128)(2,1)}), bf16[16,32,512]{2,1,0:T(8,128)(2,1)S(1)}, u32[]{:S(2)}, u32[]{:S(2)}) async-start(bf16[16,32,512]{2,1,0:T(8,128)(2,1)} %bitcast.2), calls=%async_computation | async-start | bytes 1048576 | tf_op jit(solution)/shard_map/all_to_all | solution.py:46
  12.9 10.8 %collective-permute-start = (bf16[256,512]{0,1:T(8,128)(2,1)S(1)}, bf16[256,512]{0,1:T(8,128)(2,1)}, u32[]{:S(2)}, u32[]{:S(2)}) collective-permute-start(bf16[256,512]{0,1:T(8,128)(2,1)S(1)} %dynamic-slice_select_fusion), channel_id=1, source_target_pairs={{0,8},{16,24},{33,41},{49,57},{66,74},{82,90},{99,107},{115,123},{... | collective-permute-start | bytes 786440 | tf_op jit(solution)/shard_map/ppermute | solution.py:76
  29.5 20.7 %all-to-all-start.1 = ((bf16[32,32,256]{2,1,0:T(8,128)(2,1)}), bf16[32,32,256]{2,1,0:T(8,128)(2,1)S(1)}, u32[]{:S(2)}, u32[]{:S(2)}) async-start(bf16[32,32,256]{2,1,0:T(8,128)(2,1)} %bitcast.7), calls=%async_computation.1 | async-start | bytes 1048576 | tf_op jit(solution)/shard_map/all_to_all | solution.py:109
  35.0 16.0 %collective-permute-start.1 = (bf16[512,1792]{1,0:T(8,128)(2,1)S(1)}, bf16[512,1792]{1,0:T(8,128)(2,1)}, u32[]{:S(2)}, u32[]{:S(2)}) collective-permute-start(bf16[512,1792]{1,0:T(8,128)(2,1)S(1)} %copy-done.1), channel_id=1, source_target_pairs={{0,16},{16,0},{1,17},{17,1},{2,18},{18,2},{3,19},{19,3},{4,20},{20... | collective-permute-start | bytes 5505032 | tf_op jit(solution)/shard_map/ppermute | solution.py:31
  54.0 17.1 %all-to-all-start.2 = ((bf16[4,64,1792]{2,1,0:T(8,128)(2,1)}), bf16[4,64,1792]{2,1,0:T(8,128)(2,1)S(1)}, u32[]{:S(2)}, u32[]{:S(2)}) async-start(bf16[4,64,1792]{2,1,0:T(8,128)(2,1)} %bitcast.11), calls=%async_computation.2 | async-start | bytes 1835008 | tf_op jit(solution)/shard_map/all_to_all | solution.py:46
  58.2 43.3 %copy-start.3 = (f32[16,1792]{1,0:T(8,128)S(1)}, f32[16,1792]{1,0:T(8,128)}, u32[]{:S(2)}) copy-start(f32[16,1792]{1,0:T(8,128)} %param.8) | copy-start | bytes 344068
  58.2 43.3 %copy-start.4 = (f32[16,1792]{1,0:T(8,128)S(1)}, f32[16,1792]{1,0:T(8,128)}, u32[]{:S(2)}) copy-start(f32[16,1792]{1,0:T(8,128)} %param.9) | copy-start | bytes 344068
  58.2 7.8 %collective-permute-start.2 = (bf16[256,512]{0,1:T(8,128)(2,1)S(1)}, bf16[256,512]{0,1:T(8,128)(2,1)S(1)}, u32[]{:S(2)}, u32[]{:S(2)}) collective-permute-start(bf16[256,512]{0,1:T(8,128)(2,1)S(1)} %add.166), channel_id=1, source_target_pairs={{0,2},{8,10},{16,18},{24,26},{33,35},{41,43},{49,51},{57,59},{66,6... | collective-permute-start | bytes 786440 | tf_op jit(solution)/shard_map/ppermute | solution.py:76
  66.1 5.0 %collective-permute-start.3 = (bf16[256,512]{0,1:T(8,128)(2,1)S(1)}, bf16[256,512]{0,1:T(8,128)(2,1)S(1)}, u32[]{:S(2)}, u32[]{:S(2)}) collective-permute-start(bf16[256,512]{0,1:T(8,128)(2,1)S(1)} %add.167), channel_id=1, source_target_pairs={{0,1},{8,9},{2,3},{10,11},{16,17},{24,25},{18,19},{26,27},{33,32},... | collective-permute-start | bytes 786440 | tf_op jit(solution)/shard_map/ppermute | solution.py:76
  72.0 29.6 %all-to-all-start.3 = ((bf16[4,16,1792]{2,1,0:T(8,128)(2,1)}), bf16[4,16,1792]{2,1,0:T(8,128)(2,1)S(1)}, u32[]{:S(2)}, u32[]{:S(2)}) async-start(bf16[4,16,1792]{2,1,0:T(8,128)(2,1)} %bitcast.13), calls=%async_computation.3 | async-start | bytes 458752 | tf_op jit(solution)/shard_map/all_to_all | solution.py:46
  86.7 4.6 %collective-permute-start.4 = (bf16[256,512]{0,1:T(8,128)(2,1)S(1)}, bf16[256,512]{0,1:T(8,128)(2,1)S(1)}, u32[]{:S(2)}, u32[]{:S(2)}) collective-permute-start(bf16[256,512]{0,1:T(8,128)(2,1)S(1)} %add.172), channel_id=1, source_target_pairs={{0,4},{8,12},{2,6},{10,14},{1,5},{9,13},{3,7},{11,15},{16,20},{24,... | collective-permute-start | bytes 786440 | tf_op jit(solution)/shard_map/ppermute | solution.py:76
  132.6 10.7 %collective-permute-start.5 = (bf16[256,1792]{1,0:T(8,128)(2,1)S(1)}, bf16[256,1792]{1,0:T(8,128)(2,1)S(1)}, u32[]{:S(2)}, u32[]{:S(2)}) collective-permute-start(bf16[256,1792]{1,0:T(8,128)(2,1)S(1)} %bitcast.42), channel_id=1, source_target_pairs={{0,16},{16,0},{1,17},{17,1},{2,18},{18,2},{3,19},{19,3},{4,20},{20... | collective-permute-start | bytes 2752520 | tf_op jit(solution)/shard_map/ppermute | solution.py:31

commit v3 on v2

--- a/solution.py
+++ b/solution.py
@@ -2,6 +2,9 @@
 import jax.numpy as jnp
 import numpy as np
 from jax import lax
+from jax.experimental import pallas as pl
+from jax.experimental.layout import Layout, with_layout_constraint
+from jax.experimental.pallas import tpu as pltpu
 from jax.sharding import Mesh, PartitionSpec as P
 
 STEP = 10
@@ -85,6 +88,53 @@
     return (first_next, second_next, normalized)
 
 
+def low_grad_kernel(core_ref, projected, own_cotangent, other_cotangent, out):
+    core = core_ref[0]
+    own, other = projected[core], projected[1 - core]
+    width = 256
+    for at in range(0, out.shape[1], width):
+        cols = pl.ds(at, width)
+        total = dot_rows(own, own_cotangent[:, cols]) + dot_rows(other, other_cotangent[:, cols])
+        out[:, cols] = total.astype(bf16)
+
+
+def low_grad_part(core, projected, own_cotangent, other_cotangent):
+    vmem = pl.BlockSpec(memory_space=pltpu.VMEM)
+    flops = 2 * projected.size * own_cotangent.shape[1]
+    return pl.pallas_call(
+        low_grad_kernel,
+        out_shape=jax.ShapeDtypeStruct((projected.shape[2], own_cotangent.shape[1]), bf16),
+        in_specs=[pl.BlockSpec(memory_space=pltpu.SMEM), vmem, vmem, vmem],
+        out_specs=vmem,
+        compiler_params=pltpu.CompilerParams(vmem_limit_bytes=24 << 20),
+        cost_estimate=pl.CostEstimate(flops=flops, bytes_accessed=5 << 20, transcendentals=0),
+    )(core.reshape(1), projected, own_cotangent, other_cotangent)
+
+
+def share_kernel(parts, out):
+    total = parts[0].astype(f32)
+    for i in range(1, parts.shape[0]):
+        total = total + parts[i].astype(f32)
+    mine = total.astype(bf16)
+    half = out.shape[3]
+    for c in range(2):
+        for i in range(out.shape[1]):
+            out[c, i] = mine[:, c * half : (c + 1) * half]
+
+
+def share(parts):
+    n, rows, ranks = parts.shape
+    vmem = pl.BlockSpec(memory_space=pltpu.VMEM)
+    return pl.pallas_call(
+        share_kernel,
+        out_shape=jax.ShapeDtypeStruct((2, n, rows, ranks // 2), bf16),
+        in_specs=[vmem],
+        out_specs=vmem,
+        compiler_params=pltpu.CompilerParams(vmem_limit_bytes=8 << 20),
+        cost_estimate=pl.CostEstimate(flops=parts.size, bytes_accessed=1 << 20, transcendentals=0),
+    )(parts)
+
+
 def on_device(ffn_input, up_cotangent, projector, first_moment, second_moment):
     tokens, ranks = ffn_input.shape[0], projector.shape[1]
     half = ranks // 2
@@ -98,20 +148,16 @@
     basis = lax.dynamic_slice_in_dim(ordered, core * rows, rows, 0)
     basis = jnp.where(has_rows, basis, 0)
     local = dot(ffn_input, ordered).astype(bf16)
+    local = with_layout_constraint(local, Layout((0, 1)))
     local, basis = lax.optimization_barrier((local, basis))
     came = hand_on(basis, ('x', 2))
     parts, came = lax.optimization_barrier((exchange(local, SHARD, 16), came))
     basis = basis + came
-    mine = add_up(parts).astype(bf16)
-    halves = jnp.stack([mine[:, :half], mine[:, half:]], 0)
-    halves = jnp.broadcast_to(halves[:, None], (2, 16, *halves.shape[1:]))
+    halves = share(parts)
     halves = halves.reshape(32, *halves.shape[2:])
     got = lax.all_to_all(halves, ("core", *SHARD), 0, 0)
     projected = got.reshape(2, tokens, half)
-    own = lax.dynamic_index_in_dim(projected, core, 0, False)
-    other = lax.dynamic_index_in_dim(projected, 1 - core, 0, False)
-    grad = dot_rows(own, up_cotangent) + dot_rows(other, other_cotangent)
-    grad = grad.astype(bf16)
+    grad = low_grad_part(core, projected, up_cotangent, other_cotangent)
     grad, basis = lax.optimization_barrier((grad, basis))
     basis = basis + hand_on(basis, ('z', 2))
     came = hand_on(basis, ('z', 1))

time: 145 us -> 145 us (level)
  Pallas kernels: 0 us -> 2.97 us
  matrix products: 6.55 us -> 3.58 us
    dot_general x2 -> x0, matrix products: 3.77 us -> none  [dot_rows(): lax.dot_general(a, b, (((0,), (0,)), ((), ())), preferred_element_type=f32)]
    all_to_all x1, waiting for transfers between devices: 12.1 us -> 8.34 us  [on_device(): got = lax.all_to_all(halves, ('core', *SHARD), 0, 0)]
    pallas_call x0 -> x2, Pallas kernels: none -> 2.97 us  [the longest x1 2.08 us: low_grad_part(): pl.pallas_call(low_grad_kernel, out_shape=jax.ShapeDtypeStruct((projected...]
    unnamed x10 -> x14, local copies, waits for them, and re-layouts: 0.83 us -> 3.59 us
    ppermute x2, waiting for transfers between devices: 1.55 us -> 4.05 us  [swap_cores(): return lax.ppermute(a, 'core', [(0, 1), (1, 0)])]
  transfers between devices with their start and end apart: 10 -> 10, of which waited for: 8 -> 9; matrix products, arithmetic and copies ran while one was open for 2% -> 1% of each run, Pallas kernels for 0% -> 0%
where the time goes in v3:
time: 145 us; the launch traced here: 144 us
  starting transfers between devices  56 us (39%)
  waiting for transfers between devices  44.2 us (30%)
  blocking collectives  30 us (21%)
  local copies, waits for them, and re-layouts  3.66 us (3%)
  matrix products  3.58 us (2%)
  other arithmetic  3.01 us (2%)
  Pallas kernels  2.97 us (2%)
    all_to_all x2, blocking collectives, spread(): got = lax.all_to_all(jnp.broadcast_to(a, (n, *a.shape)), axes, 0, 0)  30 us
    all_to_all x3, starting transfers between devices, exchange(): return lax.all_to_all(a.reshape(n, a.shape[0] // n, a.shape[1]), axes, 0, 0)  28.1 us
    ppermute x4, waiting for transfers between devices, hand_on(): return lax.ppermute(a, AXES, pairs)  16.7 us
    all_to_all x3, waiting for transfers between devices, exchange(): return lax.all_to_all(a.reshape(n, a.shape[0] // n, a.shape[1]), axes, 0, 0)  15.1 us
    ppermute x4, starting transfers between devices, hand_on(): return lax.ppermute(a, AXES, pairs)  11.6 us
    ppermute x2, starting transfers between devices, swap_cores(): return lax.ppermute(a, 'core', [(0, 1), (1, 0)])  11 us
    all_to_all x1, waiting for transfers between devices, on_device(): got = lax.all_to_all(halves, ('core', *SHARD), 0, 0)  8.34 us
    all_to_all x1, starting transfers between devices, on_device(): got = lax.all_to_all(halves, ('core', *SHARD), 0, 0)  5.4 us
  transfers between devices with their start and end apart: 10, of which 9 were waited for; matrix products, arithmetic and copies ran while one was open for 1% of the time, Pallas kernels for 0%

profile of v3, /device:TPU:1, one launch (start us, length us, event | category | flops | bytes accessed | tf_op | source)
XLA Modules:
  0.0 144.2 jit_solution(523254470427620587)
XLA Ops:
  0.6 0.0 copy-start
  0.6 0.0 copy-start.4
  0.7 0.2 fusion.3
  0.9 0.8 copy-done
  1.7 0.5 fusion.2
  2.2 0.0 copy-done.4
  2.2 1.3 fusion.1
  3.5 0.0 copy-start.1
  3.5 0.1 dynamic-slice_select_fusion
  3.5 9.2 %all-to-all-start = ((bf16[16,32,512]{2,1,0:T(8,128)(2,1)}), bf16[16,32,512]{2,1,0:T(8,128)(2,1)S(1)}, u32[]{:S(2)}, u32[]{:S(2)}) async-start(bf16[16,32,512]{2,1,0:T(8,128)(2,1)} %bitcast.3), calls=%async_computation | async-start | bytes 1048576 | tf_op jit(solution)/shard_map/all_to_all | solution.py:49
  12.7 5.5 %collective-permute-start = (bf16[256,512]{0,1:T(8,128)(2,1)S(1)}, bf16[256,512]{0,1:T(8,128)(2,1)}, u32[]{:S(2)}, u32[]{:S(2)}) collective-permute-start(bf16[256,512]{0,1:T(8,128)(2,1)S(1)} %dynamic-slice_select_fusion), channel_id=1, source_target_pairs={{0,8},{16,24},{33,41},{49,57},{66,74},{82,90},{99,107},{115,123},{... | collective-permute-start | bytes 786440 | tf_op jit(solution)/shard_map/ppermute | solution.py:79
  18.1 5.4 %collective-permute-done = bf16[256,512]{0,1:T(8,128)(2,1)} collective-permute-done((bf16[256,512]{0,1:T(8,128)(2,1)S(1)}, bf16[256,512]{0,1:T(8,128)(2,1)}, u32[]{:S(2)}, u32[]{:S(2)}) %collective-permute-start) | collective-permute-done | bytes 262176 | tf_op jit(solution)/shard_map/ppermute | solution.py:79
  23.5 4.9 %all-to-all-done.parts = bf16[16,32,512]{2,1,0:T(8,128)(2,1)S(1)} async-done(((bf16[16,32,512]{2,1,0:T(8,128)(2,1)}), bf16[16,32,512]{2,1,0:T(8,128)(2,1)S(1)}, u32[]{:S(2)}, u32[]{:S(2)}) %all-to-all-start) | async-done | bytes 524320 | tf_op jit(solution)/shard_map/all_to_all | solution.py:49
  28.4 0.9 shard_map.76
  29.3 5.4 %all-to-all-start.1 = ((bf16[32,32,256]{2,1,0:T(8,128)(2,1)}), bf16[32,32,256]{2,1,0:T(8,128)(2,1)S(1)}, u32[]{:S(2)}, u32[]{:S(2)}) async-start(bf16[32,32,256]{2,1,0:T(8,128)(2,1)} %bitcast.4), calls=%async_computation.1 | async-start | bytes 1048576 | tf_op jit(solution)/shard_map/all_to_all | solution.py:158
  34.7 0.0 copy-done.1
  34.7 2.2 %collective-permute-start.1 = (bf16[512,1792]{1,0:T(8,128)(2,1)S(1)}, bf16[512,1792]{1,0:T(8,128)(2,1)S(1)}, u32[]{:S(2)}, u32[]{:S(2)}) collective-permute-start(bf16[512,1792]{1,0:T(8,128)(2,1)S(1)} %copy-done.1), channel_id=1, source_target_pairs={{0,16},{16,0},{1,17},{17,1},{2,18},{18,2},{3,19},{19,3},{4,20},{20... | collective-permute-start | bytes 5505032 | tf_op jit(solution)/shard_map/ppermute | solution.py:34
  36.8 1.0 add.86
  37.9 2.5 %collective-permute-done.1.other_cotangent = bf16[512,1792]{1,0:T(8,128)(2,1)S(1)} collective-permute-done((bf16[512,1792]{1,0:T(8,128)(2,1)S(1)}, bf16[512,1792]{1,0:T(8,128)(2,1)S(1)}, u32[]{:S(2)}, u32[]{:S(2)}) %collective-permute-start.1) | collective-permute-done | bytes 1835040 | tf_op jit(solution)/shard_map/ppermute | solution.py:34
  40.4 1.3 copy-done.2
  41.6 8.3 %all-to-all-done.1 = bf16[32,32,256]{2,1,0:T(8,128)(2,1)S(1)} async-done(((bf16[32,32,256]{2,1,0:T(8,128)(2,1)}), bf16[32,32,256]{2,1,0:T(8,128)(2,1)S(1)}, u32[]{:S(2)}, u32[]{:S(2)}) %all-to-all-start.1) | async-done | bytes 524320 | tf_op jit(solution)/shard_map/all_to_all | solution.py:158
  50.0 0.0 copy-start.3
  50.0 1.5 %copy-done.3 = bf16[512,1792]{1,0:T(8,128)(2,1)S(1)} copy-done((bf16[512,1792]{1,0:T(8,128)(2,1)S(1)}, bf16[512,1792]{1,0:T(8,128)(2,1)}, u32[]{:S(2)}) %copy-start.3) | copy-done | bytes 1835032
  51.5 2.1 %shard_map.77 = bf16[256,1792]{1,0:T(8,128)(2,1)} custom-call(s32[1]{0:T(128)} %bitcast.core_ref, bf16[2,512,256]{2,1,0:T(8,128)(2,1)S(1)} %bitcast.26, bf16[512,1792]{1,0:T(8,128)(2,1)S(1)} %copy-done.1, bf16[512,1792]{1,0:T(8,128)(2,1)S(1)} %copy-done.3), custom_call_target="tpu_custom_call" | custom-call | flops 939524096 | bytes 5242880 | tf_op jit(solution)/shard_map/pallas_call | solution.py:104
  53.5 4.2 %all-to-all-start.2 = ((bf16[4,64,1792]{2,1,0:T(8,128)(2,1)}), bf16[4,64,1792]{2,1,0:T(8,128)(2,1)S(1)}, u32[]{:S(2)}, u32[]{:S(2)}) async-start(bf16[4,64,1792]{2,1,0:T(8,128)(2,1)} %bitcast.6), calls=%async_computation.2 | async-start | bytes 1835008 | tf_op jit(solution)/shard_map/all_to_all | solution.py:49
  57.7 3.5 %collective-permute-start.2 = (bf16[256,512]{0,1:T(8,128)(2,1)S(1)}, bf16[256,512]{0,1:T(8,128)(2,1)S(1)}, u32[]{:S(2)}, u32[]{:S(2)}) collective-permute-start(bf16[256,512]{0,1:T(8,128)(2,1)S(1)} %add.86), channel_id=1, source_target_pairs={{0,2},{8,10},{16,18},{24,26},{33,35},{41,43},{49,51},{57,59},{66,6... | collective-permute-start | bytes 786440 | tf_op jit(solution)/shard_map/ppermute | solution.py:79
  61.2 4.3 %collective-permute-done.2 = bf16[256,512]{0,1:T(8,128)(2,1)S(1)} collective-permute-done((bf16[256,512]{0,1:T(8,128)(2,1)S(1)}, bf16[256,512]{0,1:T(8,128)(2,1)S(1)}, u32[]{:S(2)}, u32[]{:S(2)}) %collective-permute-start.2) | collective-permute-done | bytes 262176 | tf_op jit(solution)/shard_map/ppermute | solution.py:79
  65.6 0.1 add.87
  65.6 1.3 collective-permute-start.3
  66.9 3.7 %collective-permute-done.3 = bf16[256,512]{0,1:T(8,128)(2,1)S(1)} collective-permute-done((bf16[256,512]{0,1:T(8,128)(2,1)S(1)}, bf16[256,512]{0,1:T(8,128)(2,1)S(1)}, u32[]{:S(2)}, u32[]{:S(2)}) %collective-permute-start.3) | collective-permute-done | bytes 262176 | tf_op jit(solution)/shard_map/ppermute | solution.py:79
  70.6 0.0 all-to-all-done.2
  70.6 0.8 fusion.5
  71.4 0.1 add.92
  71.5 14.7 %all-to-all-start.3 = ((bf16[4,16,1792]{2,1,0:T(8,128)(2,1)}), bf16[4,16,1792]{2,1,0:T(8,128)(2,1)S(1)}, u32[]{:S(2)}, u32[]{:S(2)}) async-start(bf16[4,16,1792]{2,1,0:T(8,128)(2,1)} %bitcast.8), calls=%async_computation.3 | async-start | bytes 458752 | tf_op jit(solution)/shard_map/all_to_all | solution.py:49
  86.2 1.3 collective-permute-start.4
  87.5 3.3 %collective-permute-done.4 = bf16[256,512]{0,1:T(8,128)(2,1)S(1)} collective-permute-done((bf16[256,512]{0,1:T(8,128)(2,1)S(1)}, bf16[256,512]{0,1:T(8,128)(2,1)S(1)}, u32[]{:S(2)}, u32[]{:S(2)}) %collective-permute-start.4) | collective-permute-done | bytes 262176 | tf_op jit(solution)/shard_map/ppermute | solution.py:79
  90.8 10.3 %all-to-all-done.3 = bf16[4,16,1792]{2,1,0:T(8,128)(2,1)S(1)} async-done(((bf16[4,16,1792]{2,1,0:T(8,128)(2,1)}), bf16[4,16,1792]{2,1,0:T(8,128)(2,1)S(1)}, u32[]{:S(2)}, u32[]{:S(2)}) %all-to-all-start.3) | async-done | bytes 229408 | tf_op jit(solution)/shard_map/all_to_all | solution.py:49
  101.1 0.0 copy-done.5
  101.1 0.0 copy-done.6
  101.1 0.8 divide_convert_fusion
  101.9 18.5 %all_to_all.30 = bf16[4,16,1792]{2,1,0:T(8,128)(2,1)S(1)} all-to-all(bf16[4,16,1792]{2,1,0:T(8,128)(2,1)S(1)} %broadcast_in_dim.11), channel_id=1, replica_groups=mesh['y'=4,'zh'=4,'core'=2,'x'=4,'zl'=4] {'zh'}, dimensions={0} | all-to-all | bytes 458752 | tf_op jit(solution)/shard_map/all_to_all | solution.py:60
  120.4 0.1 broadcast_in_dim.12
  120.4 11.5 %all_to_all.31 = bf16[4,64,1792]{2,1,0:T(8,128)(2,1)S(1)} all-to-all(bf16[4,64,1792]{2,1,0:T(8,128)(2,1)S(1)} %broadcast_in_dim.12), channel_id=1, replica_groups=mesh['y'=4,'zh'=4,'core'=2,'x'=4,'zl'=4] {'y'}, dimensions={0} | all-to-all | bytes 1835008 | tf_op jit(solution)/shard_map/all_to_all | solution.py:60
  131.9 8.8 %collective-permute-start.5 = (bf16[256,1792]{1,0:T(8,128)(2,1)S(1)}, bf16[256,1792]{1,0:T(8,128)(2,1)S(1)}, u32[]{:S(2)}, u32[]{:S(2)}) collective-permute-start(bf16[256,1792]{1,0:T(8,128)(2,1)S(1)} %bitcast.27), channel_id=1, source_target_pairs={{0,16},{16,0},{1,17},{17,1},{2,18},{18,2},{3,19},{19,3},{4,20},{20... | collective-permute-start | bytes 2752520 | tf_op jit(solution)/shard_map/ppermute | solution.py:34
  140.7 0.1 add.93
  140.8 0.5 fusion.7
  141.3 1.5 %collective-permute-done.5 = bf16[256,1792]{1,0:T(8,128)(2,1)S(1)} collective-permute-done((bf16[256,1792]{1,0:T(8,128)(2,1)S(1)}, bf16[256,1792]{1,0:T(8,128)(2,1)S(1)}, u32[]{:S(2)}, u32[]{:S(2)}) %collective-permute-start.5) | collective-permute-done | bytes 917536 | tf_op jit(solution)/shard_map/ppermute | solution.py:34
  142.8 1.4 fusion
  (7 shorter events, 0.0 us)
Async XLA Ops:
  0.6 1.0 copy-start
  0.6 1.5 %copy-start.4 = (bf16[512,512]{1,0:T(8,128)(2,1)S(1)}, bf16[512,512]{1,0:T(8,128)(2,1)}, u32[]{:S(2)}) copy-start(bf16[512,512]{1,0:T(8,128)(2,1)} %param.5) | copy-start | bytes 1572868
  3.5 31.2 %copy-start.1 = (bf16[512,1792]{1,0:T(8,128)(2,1)S(1)}, bf16[512,1792]{1,0:T(8,128)(2,1)}, u32[]{:S(2)}) copy-start(bf16[512,1792]{1,0:T(8,128)(2,1)} %own_cotangent.1) | copy-start | bytes 5505028
  3.5 24.9 %all-to-all-start = ((bf16[16,32,512]{2,1,0:T(8,128)(2,1)}), bf16[16,32,512]{2,1,0:T(8,128)(2,1)S(1)}, u32[]{:S(2)}, u32[]{:S(2)}) async-start(bf16[16,32,512]{2,1,0:T(8,128)(2,1)} %bitcast.3), calls=%async_computation | async-start | bytes 1048576 | tf_op jit(solution)/shard_map/all_to_all | solution.py:49
  12.7 10.8 %collective-permute-start = (bf16[256,512]{0,1:T(8,128)(2,1)S(1)}, bf16[256,512]{0,1:T(8,128)(2,1)}, u32[]{:S(2)}, u32[]{:S(2)}) collective-permute-start(bf16[256,512]{0,1:T(8,128)(2,1)S(1)} %dynamic-slice_select_fusion), channel_id=1, source_target_pairs={{0,8},{16,24},{33,41},{49,57},{66,74},{82,90},{99,107},{115,123},{... | collective-permute-start | bytes 786440 | tf_op jit(solution)/shard_map/ppermute | solution.py:79
  29.3 20.7 %all-to-all-start.1 = ((bf16[32,32,256]{2,1,0:T(8,128)(2,1)}), bf16[32,32,256]{2,1,0:T(8,128)(2,1)S(1)}, u32[]{:S(2)}, u32[]{:S(2)}) async-start(bf16[32,32,256]{2,1,0:T(8,128)(2,1)} %bitcast.4), calls=%async_computation.1 | async-start | bytes 1048576 | tf_op jit(solution)/shard_map/all_to_all | solution.py:158
  34.7 5.7 %collective-permute-start.1 = (bf16[512,1792]{1,0:T(8,128)(2,1)S(1)}, bf16[512,1792]{1,0:T(8,128)(2,1)S(1)}, u32[]{:S(2)}, u32[]{:S(2)}) collective-permute-start(bf16[512,1792]{1,0:T(8,128)(2,1)S(1)} %copy-done.1), channel_id=1, source_target_pairs={{0,16},{16,0},{1,17},{17,1},{2,18},{18,2},{3,19},{19,3},{4,20},{20... | collective-permute-start | bytes 5505032 | tf_op jit(solution)/shard_map/ppermute | solution.py:34
  40.4 1.3 copy-start.2
  50.0 1.5 %copy-start.3 = (bf16[512,1792]{1,0:T(8,128)(2,1)S(1)}, bf16[512,1792]{1,0:T(8,128)(2,1)}, u32[]{:S(2)}) copy-start(bf16[512,1792]{1,0:T(8,128)(2,1)} %copy-done.2) | copy-start | bytes 5505028
  53.5 17.1 %all-to-all-start.2 = ((bf16[4,64,1792]{2,1,0:T(8,128)(2,1)}), bf16[4,64,1792]{2,1,0:T(8,128)(2,1)S(1)}, u32[]{:S(2)}, u32[]{:S(2)}) async-start(bf16[4,64,1792]{2,1,0:T(8,128)(2,1)} %bitcast.6), calls=%async_computation.2 | async-start | bytes 1835008 | tf_op jit(solution)/shard_map/all_to_all | solution.py:49
  57.7 43.3 %copy-start.5 = (f32[16,1792]{1,0:T(8,128)S(1)}, f32[16,1792]{1,0:T(8,128)}, u32[]{:S(2)}) copy-start(f32[16,1792]{1,0:T(8,128)} %param.8) | copy-start | bytes 344068
  57.7 43.3 %copy-start.6 = (f32[16,1792]{1,0:T(8,128)S(1)}, f32[16,1792]{1,0:T(8,128)}, u32[]{:S(2)}) copy-start(f32[16,1792]{1,0:T(8,128)} %param.9) | copy-start | bytes 344068
  57.7 7.8 %collective-permute-start.2 = (bf16[256,512]{0,1:T(8,128)(2,1)S(1)}, bf16[256,512]{0,1:T(8,128)(2,1)S(1)}, u32[]{:S(2)}, u32[]{:S(2)}) collective-permute-start(bf16[256,512]{0,1:T(8,128)(2,1)S(1)} %add.86), channel_id=1, source_target_pairs={{0,2},{8,10},{16,18},{24,26},{33,35},{41,43},{49,51},{57,59},{66,6... | collective-permute-start | bytes 786440 | tf_op jit(solution)/shard_map/ppermute | solution.py:79
  65.6 5.0 %collective-permute-start.3 = (bf16[256,512]{0,1:T(8,128)(2,1)S(1)}, bf16[256,512]{0,1:T(8,128)(2,1)S(1)}, u32[]{:S(2)}, u32[]{:S(2)}) collective-permute-start(bf16[256,512]{0,1:T(8,128)(2,1)S(1)} %add.87), channel_id=1, source_target_pairs={{0,1},{8,9},{2,3},{10,11},{16,17},{24,25},{18,19},{26,27},{33,32},... | collective-permute-start | bytes 786440 | tf_op jit(solution)/shard_map/ppermute | solution.py:79
  71.5 29.6 %all-to-all-start.3 = ((bf16[4,16,1792]{2,1,0:T(8,128)(2,1)}), bf16[4,16,1792]{2,1,0:T(8,128)(2,1)S(1)}, u32[]{:S(2)}, u32[]{:S(2)}) async-start(bf16[4,16,1792]{2,1,0:T(8,128)(2,1)} %bitcast.8), calls=%async_computation.3 | async-start | bytes 458752 | tf_op jit(solution)/shard_map/all_to_all | solution.py:49
  86.2 4.6 %collective-permute-start.4 = (bf16[256,512]{0,1:T(8,128)(2,1)S(1)}, bf16[256,512]{0,1:T(8,128)(2,1)S(1)}, u32[]{:S(2)}, u32[]{:S(2)}) collective-permute-start(bf16[256,512]{0,1:T(8,128)(2,1)S(1)} %add.92), channel_id=1, source_target_pairs={{0,4},{8,12},{2,6},{10,14},{1,5},{9,13},{3,7},{11,15},{16,20},{24,... | collective-permute-start | bytes 786440 | tf_op jit(solution)/shard_map/ppermute | solution.py:79
  131.9 10.9 %collective-permute-start.5 = (bf16[256,1792]{1,0:T(8,128)(2,1)S(1)}, bf16[256,1792]{1,0:T(8,128)(2,1)S(1)}, u32[]{:S(2)}, u32[]{:S(2)}) collective-permute-start(bf16[256,1792]{1,0:T(8,128)(2,1)S(1)} %bitcast.27), channel_id=1, source_target_pairs={{0,16},{16,0},{1,17},{17,1},{2,18},{18,2},{3,19},{19,3},{4,20},{20... | collective-permute-start | bytes 2752520 | tf_op jit(solution)/shard_map/ppermute | solution.py:34
